TPU v7x, 128 devices: a whole 4x4x4 slice. The times are simulated.
128 devices in a mesh: frame: 8 (over z, core), band: 16 (over x, y).
Axes of the slice: x: 4, y: 4, z: 4, core: 2. Of those that a mesh axis runs over, the one named last changes fastest.
Arguments:
- queries: bfloat16 [16, 2048, 3072], P('frame', 'band'), may hold values from -6 to 6
- keys: bfloat16 [16, 2048, 3072], P('frame', 'band'), may hold values from -6 to 6
- values: bfloat16 [16, 2048, 3072], P('frame', 'band'), may hold values from -6 to 6
- head_kind: int32 [24], replicated, may hold values from 0 to 1, as said below
- spatial_mask: int32 [16, 16, 16], P('frame', 'band'), may hold values from 0 to 1, as said below
- temporal_mask: int32 [16, 16, 16], P('band', 'frame'), may hold values from 0 to 1, as said below
Outputs:
- attended: bfloat16 [16, 2048, 3072], P('frame', 'band')
Inputs may be any that keep to these rules, and one draw needn't show every extreme that they name: `head_kind`: exactly 16 entries are 1. `spatial_mask`: every diagonal tile (query band equal to key band) is allowed. `temporal_mask`: every diagonal tile (query frame equal to key frame) is allowed.
All inputs are finite; a program needn't handle non-finite values.
Results may differ from a plain program's by a relative error of at most 0.007.
Values may be sent and summed in bfloat16 or wider, within the bound.
A program may use at most 128 MiB of HBM per device.

v0:
```python
import math

import jax
import jax.numpy as jnp
from jax import lax
from jax.sharding import PartitionSpec as P

HD = 128
SPATIAL = 16
TILE = 128


NEGATIVE = -1e30


def key_allowed(tile_mask, count):
    tiles = jnp.arange(count, dtype=jnp.int32) // TILE
    onehot = (jnp.arange(tile_mask.shape[2], dtype=jnp.int32)[:, None] == tiles[None, :]).astype(
        jnp.float32
    )
    spread = jnp.einsum("gqt,tk->gqk", tile_mask.astype(jnp.float32), onehot)
    return spread > 0.5


def attend_step(carry, query, key, value, allowed):
    running, total, summed = carry
    scores = jnp.einsum(
        "gqhd,gkhd->ghqk", query, key, preferred_element_type=jnp.float32
    ) / math.sqrt(HD)
    groups, heads, rows, width = scores.shape
    qtiles = allowed.shape[1]
    blocked = scores.reshape(groups, heads, qtiles, rows // qtiles, width)
    blocked = jnp.where(allowed[:, None, :, None, :], blocked, NEGATIVE)
    scores = blocked.reshape(groups, heads, rows, width)
    newest = jnp.maximum(running, jnp.max(scores, axis=-1))
    weights = jnp.where(scores > 0.5 * NEGATIVE, jnp.exp(scores - newest[..., None]), 0.0)
    factor = jnp.exp(running - newest)
    total = total * factor + jnp.sum(weights, axis=-1)
    product = jnp.einsum(
        "ghqk,gkhd->ghqd", weights.astype(jnp.bfloat16), value, preferred_element_type=jnp.float32
    )
    summed = summed * factor[..., None] + product
    return (newest, total, summed)


def attend_keys(carry, query, key, value, allowed):
    groups, width, heads, depth = key.shape
    block = math.gcd(width, 512)
    count = width // block
    key_blocks = jnp.moveaxis(key.reshape(groups, count, block, heads, depth), 1, 0)
    value_blocks = jnp.moveaxis(value.reshape(groups, count, block, heads, depth), 1, 0)
    mask_blocks = jnp.moveaxis(allowed.reshape(groups, allowed.shape[1], count, block), 2, 0)

    def advance(state, blocks):
        return (attend_step(state, query, blocks[0], blocks[1], blocks[2]), None)

    carry, unused = lax.scan(advance, carry, (key_blocks, value_blocks, mask_blocks))
    return carry


def start_carry(groups, heads, rows):
    return (
        jnp.full((groups, heads, rows), NEGATIVE, jnp.float32),
        jnp.zeros((groups, heads, rows), jnp.float32),
        jnp.zeros((groups, heads, rows, HD), jnp.float32),
    )


def finish(carry):
    running, total, summed = carry
    return jnp.transpose(summed / total[..., None], (0, 2, 1, 3))


def body(queries, keys, values, head_kind, spatial_mask, temporal_mask):
    frames_here, rows_here, width = queries.shape
    heads = width // HD
    later = heads - SPATIAL
    order = jnp.argsort(1 - head_kind, stable=True)
    back = jnp.argsort(order, stable=True)
    shaped = [x.reshape(frames_here, rows_here, heads, HD) for x in (queries, keys, values)]
    spat = [jnp.take(x, order[:SPATIAL], axis=2) for x in shaped]
    temp = [jnp.take(x, order[SPATIAL:], axis=2) for x in shaped]
    key_flat = spat[1].reshape(frames_here, rows_here, SPATIAL * HD)
    value_flat = spat[2].reshape(frames_here, rows_here, SPATIAL * HD)
    piece = (
        lax.all_gather(key_flat, "band", axis=1, tiled=True),
        lax.all_gather(value_flat, "band", axis=1, tiled=True),
    )
    count = piece[0].shape[1]
    allowed = key_allowed(spatial_mask, count)
    key_part = piece[0].reshape(frames_here, count, SPATIAL, HD)
    value_part = piece[1].reshape(frames_here, count, SPATIAL, HD)
    carry = attend_keys(
        start_carry(frames_here, SPATIAL, rows_here), spat[0], key_part, value_part, allowed
    )
    out_spatial = finish(carry).astype(jnp.bfloat16)
    query_line = temp[0].reshape(1, frames_here * rows_here, later, HD)
    key_flat = temp[1].reshape(frames_here, rows_here, later * HD)
    value_flat = temp[2].reshape(frames_here, rows_here, later * HD)
    piece = (
        lax.all_gather(key_flat, "frame", axis=0, tiled=True),
        lax.all_gather(value_flat, "frame", axis=0, tiled=True),
    )
    count = piece[0].shape[0]
    allowed = key_allowed(temporal_mask, count * rows_here)
    key_part = piece[0].reshape(1, count * rows_here, later, HD)
    value_part = piece[1].reshape(1, count * rows_here, later, HD)
    carry = attend_keys(
        start_carry(1, later, frames_here * rows_here), query_line, key_part, value_part, allowed
    )
    out_temporal = finish(carry).reshape(frames_here, rows_here, later, HD).astype(jnp.bfloat16)
    joined = jnp.concatenate([out_spatial, out_temporal], axis=2)
    joined = jnp.take(joined, back, axis=2)
    return joined.reshape(frames_here, rows_here, width)


def solution(mesh):
    return jax.shard_map(
        body,
        mesh=mesh,
        in_specs=(
            P("frame", "band", None),
            P("frame", "band", None),
            P("frame", "band", None),
            P(),
            P("frame", "band", None),
            P("band", "frame", None),
        ),
        out_specs=P("frame", "band", None),
        check_vma=False,
    )
```

profile of v0, /device:TPU:0, one launch (start us, length us, event | category | flops | bytes accessed | tf_op | source)
XLA Modules:
  0.0 485.5 jit_solution(18415054827684386605)
XLA Ops:
  7.2 1.6 sort.31
  8.9 1.9 copy.58
  11.7 1.9 copy.62
  13.6 1.6 copy.63
  15.2 1.4 gather_fusion.4
  16.6 2.8 gather_fusion.5
  19.5 1.9 copy.64
  21.4 1.6 copy.65
  22.9 2.1 gather_fusion.6
  25.0 2.5 select_bitcast_fusion.3
  27.5 2.2 copy.73
  29.7 2.0 copy.74
  31.8 2.1 copy.77
  33.8 2.0 copy.78
  36.0 1.6 gather_fusion.1
  37.6 1.7 gather_fusion.2
  39.3 2.2 gather_fusion.3
  41.5 3.1 select_bitcast_fusion
  44.5 2.4 copy.66
  47.2 2.3 copy.60
  49.7 1.6 sort.32
  51.8 14.9 %all-gather.9.cloned.1.call-done = bf16[16,128,1024]{2,1,0:T(8,128)(2,1)} async-done(((bf16[2,128,1024]{2,1,0:T(8,128)(2,1)}), bf16[16,128,1024]{2,1,0:T(8,128)(2,1)}) %all-gather.9.cloned.1.call-update) | async-done | bytes 4194320 | tf_op jit(solution)/shard_map/all_gather | solution.py:101
  66.7 5.2 %copy.92 = bf16[256,8,8,128]{3,2,1,0:T(8,128)(2,1)} copy(bf16[256,8,8,128]{3,1,2,0:T(8,128)(2,1)} %bitcast.186) | data formatting | bytes 8388608
  71.9 28.7 %all-gather.11.cloned.1.call-done = bf16[16,128,1024]{2,1,0:T(8,128)(2,1)} async-done(((bf16[2,128,1024]{2,1,0:T(8,128)(2,1)}), bf16[16,128,1024]{2,1,0:T(8,128)(2,1)}) %all-gather.11.cloned.1.call-update) | async-done | bytes 4194320 | tf_op jit(solution)/shard_map/all_gather | solution.py:102
  100.6 5.3 %copy.93 = bf16[256,8,8,128]{3,2,1,0:T(8,128)(2,1)} copy(bf16[256,8,8,128]{3,1,2,0:T(8,128)(2,1)} %bitcast.187) | data formatting | bytes 8388608
  105.8 50.4 %while.31 = (s32[]{:T(128)}, f32[1,8,256]{2,1,0:T(8,128)S(1)}, f32[1,8,256]{2,1,0:T(8,128)S(1)}, f32[1,8,256,128]{3,2,1,0:T(8,128)}, pred[4,1,2,512]{3,2,1,0:T(4...) while((s32[]{:T(128)}, f32[1,8,256]{2,1,0:T(8,128)S(1)}, ...), condition=%wide.region_9.12_spmd.clone, body=%wide.region_6.11_spmd.clone.sunk | while | flops 553398272 | bytes 39193748 | solution.py:57
  105.8 1.7 constant_dynamic-slice_fusion.3
  107.9 3.8 fusion.78
  111.7 5.6 %fusion.81 = f32[1,8,256,128]{3,2,1,0:T(8,128)} fusion(f32[8,512,256]{2,1,0:T(8,128)} %get-tuple-element.370, f32[8,256]{1,0:T(8,128)S(1)} %bitcast.190, pred[256,512]{0,1:T(8,128)(4,1)S(1)} %copy.108, bf16[1,1,512,8,128]{4,3,2,0,1:T(8,128)(2,1)S(1)} %get-tuple-element.371, f32[1,8,256,128]{3,2,1,0:T(8,128)} %get-tuple-element.416, ...), kind=kOutput, calls=%fused_computation.48.clone.1 | convolution fusion | flops 275513344 | bytes 7487489 | tf_op jit(solution)/shard_map/while/body/eval_jaxpr/ghqk,gkhd->ghqd/dot_general | solution.py:39
  117.2 1.1 fusion.80
  118.4 1.7 constant_dynamic-slice_fusion.3
  120.5 3.8 fusion.78
  124.3 5.6 %fusion.81 = f32[1,8,256,128]{3,2,1,0:T(8,128)} fusion(f32[8,512,256]{2,1,0:T(8,128)} %get-tuple-element.370, f32[8,256]{1,0:T(8,128)S(1)} %bitcast.190, pred[256,512]{0,1:T(8,128)(4,1)S(1)} %copy.108, bf16[1,1,512,8,128]{4,3,2,0,1:T(8,128)(2,1)S(1)} %get-tuple-element.371, f32[1,8,256,128]{3,2,1,0:T(8,128)} %get-tuple-element.416, ...), kind=kOutput, calls=%fused_computation.48.clone.1 | convolution fusion | flops 275513344 | bytes 7487489 | tf_op jit(solution)/shard_map/while/body/eval_jaxpr/ghqk,gkhd->ghqd/dot_general | solution.py:39
  129.9 1.1 fusion.80
  131.1 1.7 constant_dynamic-slice_fusion.3
  133.1 3.8 fusion.78
  137.0 5.4 %fusion.81 = f32[1,8,256,128]{3,2,1,0:T(8,128)} fusion(f32[8,512,256]{2,1,0:T(8,128)} %get-tuple-element.370, f32[8,256]{1,0:T(8,128)S(1)} %bitcast.190, pred[256,512]{0,1:T(8,128)(4,1)S(1)} %copy.108, bf16[1,1,512,8,128]{4,3,2,0,1:T(8,128)(2,1)S(1)} %get-tuple-element.371, f32[1,8,256,128]{3,2,1,0:T(8,128)} %get-tuple-element.416, ...), kind=kOutput, calls=%fused_computation.48.clone.1 | convolution fusion | flops 275513344 | bytes 7487489 | tf_op jit(solution)/shard_map/while/body/eval_jaxpr/ghqk,gkhd->ghqd/dot_general | solution.py:39
  142.4 1.1 fusion.80
  143.6 1.7 constant_dynamic-slice_fusion.3
  145.6 3.8 fusion.78
  149.4 5.6 %fusion.81 = f32[1,8,256,128]{3,2,1,0:T(8,128)} fusion(f32[8,512,256]{2,1,0:T(8,128)} %get-tuple-element.370, f32[8,256]{1,0:T(8,128)S(1)} %bitcast.190, pred[256,512]{0,1:T(8,128)(4,1)S(1)} %copy.108, bf16[1,1,512,8,128]{4,3,2,0,1:T(8,128)(2,1)S(1)} %get-tuple-element.371, f32[1,8,256,128]{3,2,1,0:T(8,128)} %get-tuple-element.416, ...), kind=kOutput, calls=%fused_computation.48.clone.1 | convolution fusion | flops 275513344 | bytes 7487489 | tf_op jit(solution)/shard_map/while/body/eval_jaxpr/ghqk,gkhd->ghqd/dot_general | solution.py:39
  155.1 1.1 fusion.80
  156.3 2.4 divide_convert_fusion.1
  158.7 64.7 %all-gather.7.cloned.1.call-done = bf16[2,2048,2048]{1,2,0:T(8,128)(2,1)} async-done(((bf16[2,128,2048]{1,2,0:T(8,128)(2,1)}), bf16[2,2048,2048]{1,2,0:T(8,128)(2,1)}) %all-gather.7.cloned.1.call-update) | async-done | bytes 16777232 | tf_op jit(solution)/shard_map/all_gather | solution.py:87
  223.4 28.1 %reshape.224 = bf16[2,4,512,16,128]{2,1,4,3,0:T(4,128)(2,1)} reshape(bf16[2,2048,2048]{1,2,0:T(8,128)(2,1)} %all-gather.7.cloned.1.call-done) | data formatting | bytes 33554432 | tf_op jit(solution)/shard_map/reshape;reshape | solution.py:51
  251.5 28.2 %copy.88 = bf16[2,4,512,16,128]{4,2,3,0,1:T(8,128)(2,1)} copy(bf16[2,4,512,16,128]{2,1,4,3,0:T(4,128)(2,1)} %reshape.224) | data formatting | bytes 33554432 | tf_op jit(solution)/shard_map/transpose | solution.py:51
  279.7 66.1 %all-gather.5.cloned.1.call-done = bf16[2,2048,2048]{1,2,0:T(8,128)(2,1)} async-done(((bf16[2,128,2048]{1,2,0:T(8,128)(2,1)}), bf16[2,2048,2048]{1,2,0:T(8,128)(2,1)}) %all-gather.5.cloned.1.call-update) | async-done | bytes 16777232 | tf_op jit(solution)/shard_map/all_gather | solution.py:86
  345.7 27.8 %reshape.223 = bf16[2,4,512,16,128]{2,1,4,3,0:T(4,128)(2,1)} reshape(bf16[2,2048,2048]{1,2,0:T(8,128)(2,1)} %all-gather.5.cloned.1.call-done) | data formatting | bytes 33554432 | tf_op jit(solution)/shard_map/reshape;reshape | solution.py:50
  373.5 28.0 %copy.86 = bf16[2,4,512,16,128]{4,2,3,0,1:T(8,128)(2,1)} copy(bf16[2,4,512,16,128]{2,1,4,3,0:T(4,128)(2,1)} %reshape.223) | data formatting | bytes 33554432 | tf_op jit(solution)/shard_map/transpose | solution.py:50
  401.6 73.2 %while.30 = (s32[]{:T(128)}, f32[2,16,128]{2,1,0:T(8,128)S(1)}, f32[2,16,128]{2,1,0:T(8,128)S(1)}, f32[2,16,128,128]{3,2,1,0:T(8,128)S(1)}, pred[4,2,1,512]{3,1,...) while((s32[]{:T(128)}, f32[2,16,128]{2,1,0:T(8,128)S(1)}, ...), condition=%wide.region_5.7_spmd.clone, body=%wide.region_2.6_spmd.clone.sunk | while | flops 1106792448 | bytes 72620176 | solution.py:57
  401.6 6.9 %bitcast_reduce_fusion.2 = (f32[2,16,128]{2,1,0:T(8,128)S(1)}, f32[2,16,512,128]{3,2,1,0:T(8,128)}) fusion(pred[2,512]{1,0:T(4,128)(4,1)S(1)} %dynamic-slice_bitcast_fusion.4, bf16[2,128,16,128]{3,1,2,0:T(8,128)(2,1)S(1)} %get-tuple-element.399, bf16[4,2,512,16,128]{4,2,3,1,0:T(8,128)(2,1)} %get-tuple-element.398, s32[]{:T(128)} %get-tuple-element.383), kind=kOutput, calls=%fused_computation.9.clone.1 | convolution fusion | flops 543158272 | bytes 13649408 | tf_op jit(solution)/shard_map/while/body/eval_jaxpr/gqhd,gkhd->ghqk/dot_general | solution.py:27
  408.5 5.5 %fusion.74 = f32[2,16,128]{2,1,0:T(8,128)S(1)} fusion(f32[2,16,512,128]{3,2,1,0:T(8,128)} %get-tuple-element.356, f32[2,16,128]{2,1,0:T(8,128)S(1)} %select_maximum_fusion.2, pred[2,512]{1,0:T(4,128)(4,1)S(1)} %dynamic-slice_bitcast_fusion.4), kind=kLoop, calls=%fused_computation.14.clone.1 | loop fusion | flops 12578816 | bytes 8422400 | tf_op jit(solution)/shard_map/while/body/eval_jaxpr/reduce_sum | solution.py:38
  414.4 5.5 %fusion.76 = f32[2,16,128,128]{3,2,1,0:T(8,128)S(1)} fusion(f32[2,16,128,128]{3,2,1,0:T(8,128)S(1)} %get-tuple-element.386, bf16[4,2,512,16,128]{4,2,3,1,0:T(8,128)(2,1)} %get-tuple-element.400, s32[]{:T(128)} %get-tuple-element.383, f32[2,16,512,128]{3,2,1,0:T(8,128)S(1)} %copy-done, f32[2,16,128]{2,1,0:T(8,128)S(1)} %select_maximum_fusion.2, ...), kind=kOutput, calls=%fused_computation.28.clone.1 | convolution fusion | flops 551026688 | bytes 16811520 | tf_op jit(solution)/shard_map/while/body/eval_jaxpr/ghqk,gkhd->ghqd/dot_general | solution.py:39
  419.9 6.9 %bitcast_reduce_fusion.2 = (f32[2,16,128]{2,1,0:T(8,128)S(1)}, f32[2,16,512,128]{3,2,1,0:T(8,128)}) fusion(pred[2,512]{1,0:T(4,128)(4,1)S(1)} %dynamic-slice_bitcast_fusion.4, bf16[2,128,16,128]{3,1,2,0:T(8,128)(2,1)S(1)} %get-tuple-element.399, bf16[4,2,512,16,128]{4,2,3,1,0:T(8,128)(2,1)} %get-tuple-element.398, s32[]{:T(128)} %get-tuple-element.383), kind=kOutput, calls=%fused_computation.9.clone.1 | convolution fusion | flops 543158272 | bytes 13649408 | tf_op jit(solution)/shard_map/while/body/eval_jaxpr/gqhd,gkhd->ghqk/dot_general | solution.py:27
  426.8 5.5 %fusion.74 = f32[2,16,128]{2,1,0:T(8,128)S(1)} fusion(f32[2,16,512,128]{3,2,1,0:T(8,128)} %get-tuple-element.356, f32[2,16,128]{2,1,0:T(8,128)S(1)} %select_maximum_fusion.2, pred[2,512]{1,0:T(4,128)(4,1)S(1)} %dynamic-slice_bitcast_fusion.4), kind=kLoop, calls=%fused_computation.14.clone.1 | loop fusion | flops 12578816 | bytes 8422400 | tf_op jit(solution)/shard_map/while/body/eval_jaxpr/reduce_sum | solution.py:38
  432.6 5.5 %fusion.76 = f32[2,16,128,128]{3,2,1,0:T(8,128)S(1)} fusion(f32[2,16,128,128]{3,2,1,0:T(8,128)S(1)} %get-tuple-element.386, bf16[4,2,512,16,128]{4,2,3,1,0:T(8,128)(2,1)} %get-tuple-element.400, s32[]{:T(128)} %get-tuple-element.383, f32[2,16,512,128]{3,2,1,0:T(8,128)S(1)} %copy-done, f32[2,16,128]{2,1,0:T(8,128)S(1)} %select_maximum_fusion.2, ...), kind=kOutput, calls=%fused_computation.28.clone.1 | convolution fusion | flops 551026688 | bytes 16811520 | tf_op jit(solution)/shard_map/while/body/eval_jaxpr/ghqk,gkhd->ghqd/dot_general | solution.py:39
  438.2 6.9 %bitcast_reduce_fusion.2 = (f32[2,16,128]{2,1,0:T(8,128)S(1)}, f32[2,16,512,128]{3,2,1,0:T(8,128)}) fusion(pred[2,512]{1,0:T(4,128)(4,1)S(1)} %dynamic-slice_bitcast_fusion.4, bf16[2,128,16,128]{3,1,2,0:T(8,128)(2,1)S(1)} %get-tuple-element.399, bf16[4,2,512,16,128]{4,2,3,1,0:T(8,128)(2,1)} %get-tuple-element.398, s32[]{:T(128)} %get-tuple-element.383), kind=kOutput, calls=%fused_computation.9.clone.1 | convolution fusion | flops 543158272 | bytes 13649408 | tf_op jit(solution)/shard_map/while/body/eval_jaxpr/gqhd,gkhd->ghqk/dot_general | solution.py:27
  445.1 5.5 %fusion.74 = f32[2,16,128]{2,1,0:T(8,128)S(1)} fusion(f32[2,16,512,128]{3,2,1,0:T(8,128)} %get-tuple-element.356, f32[2,16,128]{2,1,0:T(8,128)S(1)} %select_maximum_fusion.2, pred[2,512]{1,0:T(4,128)(4,1)S(1)} %dynamic-slice_bitcast_fusion.4), kind=kLoop, calls=%fused_computation.14.clone.1 | loop fusion | flops 12578816 | bytes 8422400 | tf_op jit(solution)/shard_map/while/body/eval_jaxpr/reduce_sum | solution.py:38
  450.9 5.5 %fusion.76 = f32[2,16,128,128]{3,2,1,0:T(8,128)S(1)} fusion(f32[2,16,128,128]{3,2,1,0:T(8,128)S(1)} %get-tuple-element.386, bf16[4,2,512,16,128]{4,2,3,1,0:T(8,128)(2,1)} %get-tuple-element.400, s32[]{:T(128)} %get-tuple-element.383, f32[2,16,512,128]{3,2,1,0:T(8,128)S(1)} %copy-done, f32[2,16,128]{2,1,0:T(8,128)S(1)} %select_maximum_fusion.2, ...), kind=kOutput, calls=%fused_computation.28.clone.1 | convolution fusion | flops 551026688 | bytes 16811520 | tf_op jit(solution)/shard_map/while/body/eval_jaxpr/ghqk,gkhd->ghqd/dot_general | solution.py:39
  456.5 6.9 %bitcast_reduce_fusion.2 = (f32[2,16,128]{2,1,0:T(8,128)S(1)}, f32[2,16,512,128]{3,2,1,0:T(8,128)}) fusion(pred[2,512]{1,0:T(4,128)(4,1)S(1)} %dynamic-slice_bitcast_fusion.4, bf16[2,128,16,128]{3,1,2,0:T(8,128)(2,1)S(1)} %get-tuple-element.399, bf16[4,2,512,16,128]{4,2,3,1,0:T(8,128)(2,1)} %get-tuple-element.398, s32[]{:T(128)} %get-tuple-element.383), kind=kOutput, calls=%fused_computation.9.clone.1 | convolution fusion | flops 543158272 | bytes 13649408 | tf_op jit(solution)/shard_map/while/body/eval_jaxpr/gqhd,gkhd->ghqk/dot_general | solution.py:27
  463.4 5.5 %fusion.74 = f32[2,16,128]{2,1,0:T(8,128)S(1)} fusion(f32[2,16,512,128]{3,2,1,0:T(8,128)} %get-tuple-element.356, f32[2,16,128]{2,1,0:T(8,128)S(1)} %select_maximum_fusion.2, pred[2,512]{1,0:T(4,128)(4,1)S(1)} %dynamic-slice_bitcast_fusion.4), kind=kLoop, calls=%fused_computation.14.clone.1 | loop fusion | flops 12578816 | bytes 8422400 | tf_op jit(solution)/shard_map/while/body/eval_jaxpr/reduce_sum | solution.py:38
  469.2 5.5 %fusion.76 = f32[2,16,128,128]{3,2,1,0:T(8,128)S(1)} fusion(f32[2,16,128,128]{3,2,1,0:T(8,128)S(1)} %get-tuple-element.386, bf16[4,2,512,16,128]{4,2,3,1,0:T(8,128)(2,1)} %get-tuple-element.400, s32[]{:T(128)} %get-tuple-element.383, f32[2,16,512,128]{3,2,1,0:T(8,128)S(1)} %copy-done, f32[2,16,128]{2,1,0:T(8,128)S(1)} %select_maximum_fusion.2, ...), kind=kOutput, calls=%fused_computation.28.clone.1 | convolution fusion | flops 551026688 | bytes 16811520 | tf_op jit(solution)/shard_map/while/body/eval_jaxpr/ghqk,gkhd->ghqd/dot_general | solution.py:39
  475.5 1.1 pad_maximum_fusion
  477.5 1.5 bitcast_select_fusion.1
  (101 shorter events, 6.7 us)
Async XLA Ops:
  6.5 60.1 %all-gather.9.cloned.1.call-start = ((), (), s32[]{:S(2)}) async-start(), calls=%async_computation.2 | async-start | bytes 4718592 | tf_op jit(solution)/shard_map/all_gather | solution.py:101
  27.5 10.1 %copy-start.2 = (bf16[2,128,24,128]{3,1,2,0:T(8,128)(2,1)S(1)}, bf16[2,128,24,128]{3,1,2,0:T(8,128)(2,1)}, u32[]{:S(2)}) copy-start(bf16[2,128,24,128]{3,1,2,0:T(8,128)(2,1)} %copy.63) | copy-start | bytes 4718596
  31.7 68.8 %all-gather.11.cloned.1.call-start = ((), (), s32[]{:S(2)}) async-start(), calls=%async_computation.3 | async-start | bytes 4718592 | tf_op jit(solution)/shard_map/all_gather | solution.py:102
  35.9 187.5 %all-gather.7.cloned.1.call-start = ((), (), s32[]{:S(2)}) async-start(), calls=%async_computation.1 | async-start | bytes 17825792 | tf_op jit(solution)/shard_map/all_gather | solution.py:87
  37.6 3.8 copy-start.3
  44.5 5.1 %copy-start.4 = (bf16[2,128,16,128]{3,1,0,2:T(8,128)(2,1)S(1)}, bf16[2,128,16,128]{3,1,0,2:T(8,128)(2,1)}, u32[]{:S(2)}) copy-start(bf16[2,128,16,128]{3,1,0,2:T(8,128)(2,1)} %get-tuple-element.250) | copy-start | bytes 3145732
  44.5 5.2 %copy-start.6 = (s32[2,1,16]{2,1,0:T(1,128)S(1)}, s32[2,1,16]{2,1,0:T(1,128)}, u32[]{:S(2)}) copy-start(s32[2,1,16]{2,1,0:T(1,128)} %param.18) | copy-start | bytes 388
  44.5 6.9 %copy-start.7 = (s32[1,2,16]{2,1,0:T(2,128)S(1)}, s32[1,2,16]{2,1,0:T(2,128)}, u32[]{:S(2)}) copy-start(s32[1,2,16]{2,1,0:T(2,128)} %param.19) | copy-start | bytes 388
  47.0 298.7 %all-gather.5.cloned.1.call-start = ((), (), s32[]{:S(2)}) async-start(), calls=%async_computation | async-start | bytes 17825792 | tf_op jit(solution)/shard_map/all_gather | solution.py:86
  111.7 5.6 %copy-start.1 = (f32[8,512,256]{2,1,0:T(8,128)S(1)}, f32[8,512,256]{2,1,0:T(8,128)}, u32[]{:S(2)}) copy-start(f32[8,512,256]{2,1,0:T(8,128)} %get-tuple-element.370) | copy-start | bytes 12582916 | tf_op jit(solution)/shard_map/while
  124.3 5.6 %copy-start.1 = (f32[8,512,256]{2,1,0:T(8,128)S(1)}, f32[8,512,256]{2,1,0:T(8,128)}, u32[]{:S(2)}) copy-start(f32[8,512,256]{2,1,0:T(8,128)} %get-tuple-element.370) | copy-start | bytes 12582916 | tf_op jit(solution)/shard_map/while
  137.0 5.4 %copy-start.1 = (f32[8,512,256]{2,1,0:T(8,128)S(1)}, f32[8,512,256]{2,1,0:T(8,128)}, u32[]{:S(2)}) copy-start(f32[8,512,256]{2,1,0:T(8,128)} %get-tuple-element.370) | copy-start | bytes 12582916 | tf_op jit(solution)/shard_map/while
  149.4 5.6 %copy-start.1 = (f32[8,512,256]{2,1,0:T(8,128)S(1)}, f32[8,512,256]{2,1,0:T(8,128)}, u32[]{:S(2)}) copy-start(f32[8,512,256]{2,1,0:T(8,128)} %get-tuple-element.370) | copy-start | bytes 12582916 | tf_op jit(solution)/shard_map/while
  373.5 28.0 %copy-start.5 = (f32[2,16,128,128]{3,2,1,0:T(8,128)S(1)}, f32[2,16,128,128]{3,2,1,0:T(8,128)}, u32[]{:S(2)}) copy-start(f32[2,16,128,128]{3,2,1,0:T(8,128)} %custom-call.2) | copy-start | bytes 6291460
  408.5 5.8 %copy-start = (f32[2,16,512,128]{3,2,1,0:T(8,128)S(1)}, f32[2,16,512,128]{3,2,1,0:T(8,128)}, u32[]{:S(2)}) copy-start(f32[2,16,512,128]{3,2,1,0:T(8,128)} %get-tuple-element.356) | copy-start | bytes 25165828 | tf_op jit(solution)/shard_map/while
  426.8 5.8 %copy-start = (f32[2,16,512,128]{3,2,1,0:T(8,128)S(1)}, f32[2,16,512,128]{3,2,1,0:T(8,128)}, u32[]{:S(2)}) copy-start(f32[2,16,512,128]{3,2,1,0:T(8,128)} %get-tuple-element.356) | copy-start | bytes 25165828 | tf_op jit(solution)/shard_map/while
  445.1 5.8 %copy-start = (f32[2,16,512,128]{3,2,1,0:T(8,128)S(1)}, f32[2,16,512,128]{3,2,1,0:T(8,128)}, u32[]{:S(2)}) copy-start(f32[2,16,512,128]{3,2,1,0:T(8,128)} %get-tuple-element.356) | copy-start | bytes 25165828 | tf_op jit(solution)/shard_map/while
  463.4 5.8 %copy-start = (f32[2,16,512,128]{3,2,1,0:T(8,128)S(1)}, f32[2,16,512,128]{3,2,1,0:T(8,128)}, u32[]{:S(2)}) copy-start(f32[2,16,512,128]{3,2,1,0:T(8,128)} %get-tuple-element.356) | copy-start | bytes 25165828 | tf_op jit(solution)/shard_map/while
Sparse Core Ops, SparseCore 0:
  31.8 34.7 all-gather.8
  68.4 32.1 all-gather.10
  102.7 120.6 all-gather.6
  225.4 120.3 all-gather.4
where the time goes:
time: 489 us; the launch traced here: 485 us
  waiting for transfers between devices  174 us (36%)
  local copies, waits for them, and re-layouts  167 us (34%)
  matrix products  87.4 us (18%)
  other arithmetic  42.1 us (9%)
  between operations  13.4 us (3%)
    all_gather x1, waiting for transfers between devices, body(): lax.all_gather(key_flat, 'band', axis=1, tiled=True)  66.1 us
    all_gather x1, waiting for transfers between devices, body(): lax.all_gather(value_flat, 'band', axis=1, tiled=True)  64.7 us
    dot_general x8, matrix products, attend_step(): jnp.einsum('ghqk,gkhd->ghqd', weights.astype(jnp.bfloat16), value, prefer...  44.1 us
    dot_general x8, matrix products, attend_step(): jnp.einsum('gqhd,gkhd->ghqk', query, key, preferred_element_type=jnp.floa...  43 us
    all_gather x1, waiting for transfers between devices, body(): lax.all_gather(value_flat, 'frame', axis=0, tiled=True)  28.7 us
    transpose x1, local copies, waits for them, and re-layouts, attend_keys(): jnp.moveaxis(value.reshape(groups, count, block, heads, depth), 1, 0)  28.2 us
    another operation x1, local copies, waits for them, and re-layouts, attend_keys(): value.reshape(groups, count, block, heads, depth)  28.1 us
    transpose x1, local copies, waits for them, and re-layouts, attend_keys(): jnp.moveaxis(key.reshape(groups, count, block, heads, depth), 1, 0)  28 us
  transfers between devices with their start and end apart: 4, of which 4 were waited for; matrix products, arithmetic and copies ran while one was open for 29% of the time, Pallas kernels for 0%

commit v1 on v0

v1 whole, which is shorter than its diff:
```python
import functools
import math

import jax
import jax.numpy as jnp
from jax import lax
from jax.experimental import pallas as pl
from jax.experimental.pallas import tpu as pltpu
from jax.sharding import PartitionSpec as P

MESH = pl.DeviceIdType.MESH
HD = 128
HEADS = 24
SPATIAL = 16
TEMPORAL = HEADS - SPATIAL
TILE = 128
TILES = 16
TOKENS = TILES * TILE
NEGATIVE = -1e30
EXPONENT = math.log2(math.e) / math.sqrt(HD)
PAD = 16
QROWS = TILE + PAD
CHUNK = 512
NT = (((1,), (1,)), ((), ()))
BF16 = jnp.bfloat16
F32 = jnp.float32

BAND_STEPS = (
    (0, 0), (1, 0), (0, 3), (3, 0), (0, 1), (2, 0), (0, 2), (1, 1),
    (3, 3), (1, 3), (3, 1), (2, 1), (1, 2), (2, 3), (3, 2), (2, 2),
)
FRAME_STEPS = ((0, 0), (0, 1), (1, 0), (3, 0), (1, 1), (3, 1), (2, 0), (2, 1))


def pick(table, index):
    if isinstance(index, int):
        return table[index]
    value = jnp.int32(table[0])
    for place in range(1, len(table)):
        value = jnp.where(index == place, jnp.int32(table[place]), value)
    return value


def band_at(me, index, sign):
    dx = pick([s[0] for s in BAND_STEPS], index)
    dy = pick([s[1] for s in BAND_STEPS], index)
    return (me // 4 + 4 + sign * dx) % 4 * 4 + (me % 4 + 4 + sign * dy) % 4


def frame_at(me, index, sign):
    dz = pick([s[0] for s in FRAME_STEPS], index)
    dc = pick([s[1] for s in FRAME_STEPS], index)
    return (me // 2 + 4 + sign * dz) % 4 * 2 + (me % 2 + dc) % 2


def score_tile(query, keys, marks, scores, tops):
    running = None
    for start in range(0, TOKENS, CHUNK):
        first = start // TILE
        key = keys[pl.ds(first, CHUNK // TILE)].reshape(CHUNK, HD)
        key = jnp.concatenate([key, marks[pl.ds(start, CHUNK), :]], axis=1)
        part = lax.dot_general(query, key, NT, preferred_element_type=F32)
        scores[:, pl.ds(start, CHUNK)] = part
        for lane in range(0, CHUNK, 128):
            piece = part[:, lane : lane + 128]
            running = piece if running is None else jnp.maximum(running, piece)
    top = jnp.max(running, axis=1, keepdims=True)
    tops[...] = jnp.broadcast_to(top, tops.shape)


def value_tile(scores, tops, values):
    top = jnp.concatenate([tops[...]] * (CHUNK // 128), axis=1)
    total = None
    ones = jnp.ones((CHUNK, HD), BF16)
    for start in range(0, TOKENS, CHUNK):
        first = start // TILE
        value = values[pl.ds(first, CHUNK // TILE)].reshape(CHUNK, HD)
        value = jnp.concatenate([value, ones], axis=1)
        weights = jnp.exp2((scores[:, pl.ds(start, CHUNK)] - top) * EXPONENT).astype(BF16)
        part = jnp.dot(weights, value, preferred_element_type=F32)
        total = part if total is None else total + part
    return (total[:, :HD] / total[:, HD:]).astype(BF16)


def kernel(
    q_hbm, k_hbm, v_hbm, kind, smask, tmask,
    out,
    q_in, k_in, v_in, q_send, k_send, v_send, qt_send, kt_send, vt_send,
    q_got, k_got, v_got, o_send, o_got, marks,
    scores0, scores1, tops0, tops1, place, order,
    load_sem, send_sem, kv_sem, q_sem, o_sem, osend_sem,
):
    group = lax.axis_index("frame")
    band = lax.axis_index("band")

    barrier = pltpu.get_barrier_semaphore()
    for i in range(1, 16):
        pl.semaphore_signal(barrier, inc=1, device_id={"band": band_at(band, i, 1)}, device_id_type=MESH)
    for i in range(1, 8):
        pl.semaphore_signal(barrier, inc=1, device_id={"frame": frame_at(group, i, 1)}, device_id_type=MESH)

    loads = []
    for i, (source, target) in enumerate(((k_hbm, k_in), (v_hbm, v_in), (q_hbm, q_in))):
        for h in range(HEADS):
            pltpu.make_async_copy(source.at[:, :, pl.ds(h * HD, HD)], target.at[h], load_sem.at[i]).start()
        loads.append(pltpu.make_async_copy(target, target, load_sem.at[i]))

    before = jnp.int32(0)
    counts = []
    for h in range(HEADS):
        here = kind[h]
        place[h] = jnp.minimum(here * before + (1 - here) * (SPATIAL + h - before), HEADS - 1)
        before = before + here
        counts.append(before)

    def fill(slot, carry):
        spatial, temporal = jnp.int32(0), jnp.int32(0)
        for h in range(HEADS):
            spatial = spatial + (counts[h] <= slot).astype(jnp.int32)
            temporal = temporal + (h + 1 - counts[h] <= slot).astype(jnp.int32)
        order[slot] = jnp.minimum(spatial, HEADS - 1)

        @pl.when(slot < TEMPORAL)
        def _():
            order[SPATIAL + slot] = jnp.minimum(temporal, HEADS - 1)

        return carry

    lax.fori_loop(0, SPATIAL, fill, 0)

    lane = lax.broadcasted_iota(jnp.int32, (TILE, 128), 1)
    for t in range(TILES):
        marks[pl.ds(t * TILE, TILE), :] = jnp.where(lane == t, 1.0, 0.0).astype(BF16)

    lane = lax.broadcasted_iota(jnp.int32, (PAD, 128), 1)

    def mask_rows(read):
        rows = jnp.zeros((PAD, 128), F32)
        for t in range(TILES):
            rows = jnp.where(lane == t, (1 - read(t)).astype(F32) * NEGATIVE, rows)
        return rows.astype(BF16)

    spatial_rows = [mask_rows(lambda t, f=f: smask[f, 0, t]) for f in range(2)]
    temporal_rows = [mask_rows(lambda t, f=f: tmask[0, f, t]) for f in range(2)]

    def head(ref, f, slot):
        return ref[order[slot], f]

    def send_spatial(which, f, kind_index):
        source, staged, got = which
        query = staged is q_send
        for i in range(16):
            dest = band_at(band, i, 1)
            block = head(source, f, dest)
            if i == 0:
                got[f, band, pl.ds(0, TILE), :] = block
                if query:
                    got[f, band, pl.ds(TILE, PAD), :] = spatial_rows[f]
                continue
            staged[f, i, pl.ds(0, TILE), :] = block
            if query:
                staged[f, i, pl.ds(TILE, PAD), :] = spatial_rows[f]
            pltpu.make_async_remote_copy(
                src_ref=staged.at[f, i],
                dst_ref=got.at[f, band],
                send_sem=send_sem.at[kind_index, f],
                recv_sem=q_sem.at[f, i] if query else kv_sem.at[kind_index, f],
                device_id={"band": dest},
                device_id_type=MESH,
            ).start()

    def send_temporal(which, kind_index):
        source, staged, got = which
        query = staged is qt_send
        for i in range(8):
            dest = frame_at(group, i, 1)
            for f in range(2):
                block = head(source, f, SPATIAL + dest)
                if i == 0:
                    got[2, 2 * group + f, pl.ds(0, TILE), :] = block
                    if query:
                        got[2, 2 * group + f, pl.ds(TILE, PAD), :] = temporal_rows[f]
                else:
                    staged[i, f, pl.ds(0, TILE), :] = block
                    if query:
                        staged[i, f, pl.ds(TILE, PAD), :] = temporal_rows[f]
            if i > 0:
                pltpu.make_async_remote_copy(
                    src_ref=staged.at[i],
                    dst_ref=got.at[2, pl.ds(2 * group, 2)],
                    send_sem=send_sem.at[kind_index, 2],
                    recv_sem=q_sem.at[2, i] if query else kv_sem.at[kind_index, 2],
                    device_id={"frame": dest},
                    device_id_type=MESH,
                ).start()

    spatial_k, spatial_v, spatial_q = (k_in, k_send, k_got), (v_in, v_send, v_got), (q_in, q_send, q_got)
    temporal_k, temporal_v, temporal_q = (k_in, kt_send, k_got), (v_in, vt_send, v_got), (q_in, qt_send, q_got)

    loads[0].wait()
    pl.semaphore_wait(barrier, 22)
    send_spatial(spatial_k, 0, 0)
    send_temporal(temporal_k, 0)
    loads[1].wait()
    send_spatial(spatial_v, 0, 1)
    send_temporal(temporal_v, 1)
    loads[2].wait()
    send_spatial(spatial_q, 0, 2)
    send_temporal(temporal_q, 2)
    send_spatial(spatial_k, 1, 0)
    send_spatial(spatial_v, 1, 1)
    send_spatial(spatial_q, 1, 2)

    def wait_bytes(ref, sem):
        pltpu.make_async_copy(ref, ref, sem).wait()

    def wait_keys(u):
        many = 15 if u < 2 else 14
        wait_bytes(k_got.at[u, pl.ds(0, many)], kv_sem.at[0, u])
        wait_bytes(v_got.at[u, pl.ds(0, many)], kv_sem.at[1, u])

    def tiles_of(u, step):
        if u < 2:
            return band_at(band, 2 * step, -1), band_at(band, 2 * step + 1, -1)
        source = frame_at(group, step, -1)
        return 2 * source, 2 * source + 1

    def wait_query(u, step):
        if u < 2:

            @pl.when(step > 0)
            def _():
                wait_bytes(q_got.at[u, 0], q_sem.at[u, 2 * step])

            wait_bytes(q_got.at[u, 0], q_sem.at[u, 2 * step + 1])
        else:

            @pl.when(step > 0)
            def _():
                wait_bytes(q_got.at[u, pl.ds(0, 2)], q_sem.at[u, step])

    def run_scores(u, step, scores, tops):
        rows = []
        for t in tiles_of(u, step):
            bias = jnp.concatenate([q_got[u, t, pl.ds(TILE, PAD), :]] * (TILE // PAD), axis=0)
            rows.append(jnp.concatenate([q_got[u, t, pl.ds(0, TILE), :], bias], axis=1))
        score_tile(jnp.concatenate(rows, axis=0), k_got.at[u], marks, scores, tops)

    def run_values(u, step, scores, tops):
        result = value_tile(scores, tops, v_got.at[u])
        first, second = tiles_of(u, step)
        o_send[u, first] = result[:TILE]
        o_send[u, second] = result[TILE:]
        if u < 2:
            for t, guarded in ((first, True), (second, False)):
                copy = pltpu.make_async_remote_copy(
                    src_ref=o_send.at[u, t],
                    dst_ref=o_got.at[band, u],
                    send_sem=osend_sem.at[u],
                    recv_sem=o_sem.at[u],
                    device_id={"band": t},
                    device_id_type=MESH,
                )
                if guarded:
                    pl.when(step > 0)(copy.start)
                else:
                    copy.start()
        else:
            copy = pltpu.make_async_remote_copy(
                src_ref=o_send.at[2, pl.ds(first, 2)],
                dst_ref=o_got.at[SPATIAL + group],
                send_sem=osend_sem.at[u],
                recv_sem=o_sem.at[u],
                device_id={"frame": first // 2},
                device_id_type=MESH,
            )
            pl.when(step > 0)(copy.start)

    def run_unit(u):
        wait_keys(u)
        wait_query(u, 0)
        run_scores(u, 0, scores0, tops0)

        def body(i, carry):
            wait_query(u, 2 * i + 1)
            run_scores(u, 2 * i + 1, scores1, tops1)
            run_values(u, 2 * i, scores0, tops0)

            @pl.when(i < 3)
            def _():
                wait_query(u, 2 * i + 2)

            run_scores(u, jnp.minimum(2 * i + 2, 7), scores0, tops0)
            run_values(u, 2 * i + 1, scores1, tops1)
            return carry

        lax.fori_loop(0, 4, body, 0)

    run_unit(0)
    run_unit(2)
    run_unit(1)

    for f in range(2):
        o_got[band, f] = o_send[f, band]
        o_got[SPATIAL + group, f] = o_send[2, 2 * group + f]

    for f in range(2):
        wait_bytes(k_send.at[f, pl.ds(1, 15)], send_sem.at[0, f])
        wait_bytes(v_send.at[f, pl.ds(1, 15)], send_sem.at[1, f])
        wait_bytes(q_send.at[f, pl.ds(1, 15)], send_sem.at[2, f])
    wait_bytes(kt_send.at[pl.ds(1, 7)], send_sem.at[0, 2])
    wait_bytes(vt_send.at[pl.ds(1, 7)], send_sem.at[1, 2])
    wait_bytes(qt_send.at[pl.ds(1, 7)], send_sem.at[2, 2])
    for u, many in ((0, 15), (1, 15), (2, 14)):
        wait_bytes(o_send.at[u, pl.ds(0, many)], osend_sem.at[u])
    for u, many in ((0, 15), (1, 15), (2, 14)):
        wait_bytes(o_send.at[u, pl.ds(0, many)], o_sem.at[u])

    for h in range(HEADS):
        for f in range(2):
            out[f, :, pl.ds(h * HD, HD)] = o_got[place[h], f]


def body(queries, keys, values, head_kind, spatial_mask, temporal_mask):
    vmem, sem = pltpu.VMEM, pltpu.SemaphoreType.DMA
    hbm = pl.BlockSpec(memory_space=pl.ANY)
    smem = pl.BlockSpec(memory_space=pltpu.SMEM)
    return pl.pallas_call(
        kernel,
        out_shape=jax.ShapeDtypeStruct(queries.shape, BF16),
        in_specs=[hbm, hbm, hbm, smem, smem, smem],
        out_specs=pl.BlockSpec(memory_space=pltpu.VMEM),
        scratch_shapes=[
            vmem((HEADS, 2, TILE, HD), BF16), vmem((HEADS, 2, TILE, HD), BF16), vmem((HEADS, 2, TILE, HD), BF16),
            vmem((2, 16, QROWS, HD), BF16), vmem((2, 16, TILE, HD), BF16), vmem((2, 16, TILE, HD), BF16),
            vmem((8, 2, QROWS, HD), BF16), vmem((8, 2, TILE, HD), BF16), vmem((8, 2, TILE, HD), BF16),
            vmem((3, TILES, QROWS, HD), BF16), vmem((3, TILES, TILE, HD), BF16), vmem((3, TILES, TILE, HD), BF16),
            vmem((3, TILES, TILE, HD), BF16), vmem((HEADS, 2, TILE, HD), BF16),
            vmem((TOKENS, 128), BF16),
            vmem((256, TOKENS), F32), vmem((256, TOKENS), F32), vmem((256, 128), F32), vmem((256, 128), F32),
            pltpu.SMEM((HEADS,), jnp.int32), pltpu.SMEM((HEADS,), jnp.int32),
            sem((3,)), sem((3, 3)), sem((2, 3)), sem((3, 16)), sem((3,)), sem((3,)),
        ],
        compiler_params=pltpu.CompilerParams(
            collective_id=0, has_side_effects=True, vmem_limit_bytes=48 * 2**20
        ),
        cost_estimate=pl.CostEstimate(flops=6442450944, bytes_accessed=6291456, transcendentals=12582912),
    )(queries, keys, values, head_kind, spatial_mask, temporal_mask)


def solution(mesh):
    return jax.shard_map(
        body,
        mesh=mesh,
        in_specs=(
            P("frame", "band", None),
            P("frame", "band", None),
            P("frame", "band", None),
            P(),
            P("frame", "band", None),
            P("band", "frame", None),
        ),
        out_specs=P("frame", "band", None),
        check_vma=False,
    )
```

time: 489 us -> 65.4 us (0.13)
  waiting for transfers between devices: 174 us -> 0 us
  local copies, waits for them, and re-layouts: 167 us -> 5.97 us
  matrix products: 87.4 us -> 0 us
  Pallas kernels: 0 us -> 59 us
  other arithmetic: 42.1 us -> 0 us
  between operations: 13.4 us -> 0.01 us
    all_gather x4 -> x0, waiting for transfers between devices: 174 us -> none  [the longest x1 66.1 us: body(): lax.all_gather(key_flat, 'band', axis=1, tiled=True)]
    dot_general x18 -> x0, matrix products: 87.4 us -> none  [the longest x8 44.1 us: attend_step(): jnp.einsum('ghqk,gkhd->ghqd', weights.astype(jnp.bfloat16), value, prefer...]
    pallas_call x0 -> x1, Pallas kernels: none -> 59 us  [body(): pl.pallas_call(kernel, out_shape=jax.ShapeDtypeStruct(queries.shape, BF16...]
    transpose x2 -> x0, local copies, waits for them, and re-layouts: 56.2 us -> none  [the longest x1 28.2 us: attend_keys(): jnp.moveaxis(value.reshape(groups, count, block, heads, depth), 1, 0)]
    another operation x2 -> x0, local copies, waits for them, and re-layouts: 55.9 us -> none  [the longest x1 28.1 us: attend_keys(): value.reshape(groups, count, block, heads, depth)]
    reduce_sum x8 -> x0, other arithmetic: 26.7 us -> none  [attend_step(): total = total * factor + jnp.sum(weights, axis=-1)]
    gather x7 -> x0, local copies, waits for them, and re-layouts: 12.6 us -> none  [the longest x3 6.3 us: body(): temp = [jnp.take(x, order[SPATIAL:], axis=2) for x in shaped]]
    unnamed x18 -> x11, local copies, waits for them, and re-layouts: 16.4 us -> 5.97 us
  transfers between devices with their start and end apart: 4 -> 0, of which waited for: 4 -> 0; matrix products, arithmetic and copies ran while one was open for 29% -> 0% of each run, Pallas kernels for 0% -> 0%
where the time goes in v1:
time: 65.4 us; the launch traced here: 65 us
  Pallas kernels  59 us (90%)
  local copies, waits for them, and re-layouts  5.97 us (9%)
    pallas_call x1, Pallas kernels, body(): pl.pallas_call(kernel, out_shape=jax.ShapeDtypeStruct(queries.shape, BF16...  59 us
    unnamed x11, local copies, waits for them, and re-layouts  5.97 us

profile of v1, /device:TPU:0, one launch (start us, length us, event | category | flops | bytes accessed | tf_op | source)
XLA Modules:
  0.0 65.0 jit_solution(15982866418936110031)
XLA Ops:
  0.0 0.0 copy-start
  0.0 1.4 %copy-done = bf16[2,128,3072]{2,1,0:T(8,128)(2,1)S(1)} copy-done((bf16[2,128,3072]{2,1,0:T(8,128)(2,1)S(1)}, bf16[2,128,3072]{2,1,0:T(8,128)(2,1)}, u32[]{:S(2)}) %copy-start) | copy-done | bytes 1572888
  1.4 0.0 copy-start.1
  1.4 1.4 %copy-done.1 = bf16[2,128,3072]{2,1,0:T(8,128)(2,1)S(1)} copy-done((bf16[2,128,3072]{2,1,0:T(8,128)(2,1)S(1)}, bf16[2,128,3072]{2,1,0:T(8,128)(2,1)}, u32[]{:S(2)}) %copy-start.1) | copy-done | bytes 1572888
  2.8 0.0 copy-start.2
  2.8 0.7 %copy-done.2 = s32[2,1,16]{2,1,0:T(1,128)S(1)} copy-done((s32[2,1,16]{2,1,0:T(1,128)S(1)}, s32[2,1,16]{2,1,0:T(1,128)}, u32[]{:S(2)}) %copy-start.2) | copy-done | bytes 152
  3.5 0.0 copy-start.3
  3.5 0.7 %copy-done.3 = s32[1,2,16]{2,1,0:T(2,128)S(1)} copy-done((s32[1,2,16]{2,1,0:T(2,128)S(1)}, s32[1,2,16]{2,1,0:T(2,128)}, u32[]{:S(2)}) %copy-start.3) | copy-done | bytes 152
  4.2 0.0 copy-start.4
  4.2 0.7 %copy-done.4 = s32[24]{0:T(128)S(1)} copy-done((s32[24]{0:T(128)S(1)}, s32[24]{0:T(128)}, u32[]{:S(2)}) %copy-start.4) | copy-done | bytes 120
  4.8 59.0 %shard_map.64 = bf16[2,128,3072]{2,1,0:T(8,128)(2,1)S(1)} custom-call(bf16[2,128,3072]{2,1,0:T(8,128)(2,1)S(1)} %copy-done, bf16[2,128,3072]{2,1,0:T(8,128)(2,1)S(1)} %copy-done.1, bf16[2,128,3072]{2,1,0:T(8,128)(2,1)} %v_hbm.1, s32[24]{0:T(128)S(1)} %copy-done.4, s32[2,1,16]{2,1,0:T(1,128)S(1)} %copy-done.2, s32[1,2,16]{2,1,0:T(2,128)S(1)} %copy-done.3), custom_call_target="tpu_custom_call" | custom-call | flops 6442450944 | bytes 6291456 | tf_op jit(solution)/shard_map/pallas_call | solution.py:328
  63.8 1.1 %copy.8 = bf16[2,128,3072]{2,1,0:T(8,128)(2,1)} copy(bf16[2,128,3072]{2,1,0:T(8,128)(2,1)S(1)} %shard_map.64) | data formatting | bytes 3145728
Async XLA Ops:
  0.0 1.4 %copy-start = (bf16[2,128,3072]{2,1,0:T(8,128)(2,1)S(1)}, bf16[2,128,3072]{2,1,0:T(8,128)(2,1)}, u32[]{:S(2)}) copy-start(bf16[2,128,3072]{2,1,0:T(8,128)(2,1)} %q_hbm.1) | copy-start | bytes 4718596
  1.4 1.4 %copy-start.1 = (bf16[2,128,3072]{2,1,0:T(8,128)(2,1)S(1)}, bf16[2,128,3072]{2,1,0:T(8,128)(2,1)}, u32[]{:S(2)}) copy-start(bf16[2,128,3072]{2,1,0:T(8,128)(2,1)} %k_hbm.1) | copy-start | bytes 4718596
  2.8 0.7 %copy-start.2 = (s32[2,1,16]{2,1,0:T(1,128)S(1)}, s32[2,1,16]{2,1,0:T(1,128)}, u32[]{:S(2)}) copy-start(s32[2,1,16]{2,1,0:T(1,128)} %smask.1) | copy-start | bytes 388
  3.5 0.7 %copy-start.3 = (s32[1,2,16]{2,1,0:T(2,128)S(1)}, s32[1,2,16]{2,1,0:T(2,128)}, u32[]{:S(2)}) copy-start(s32[1,2,16]{2,1,0:T(2,128)} %tmask.1) | copy-start | bytes 388
  4.2 0.7 %copy-start.4 = (s32[24]{0:T(128)S(1)}, s32[24]{0:T(128)}, u32[]{:S(2)}) copy-start(s32[24]{0:T(128)} %kind.1) | copy-start | bytes 292

commit v2 on v1

v2 whole, which is shorter than its diff:
```python
import functools
import math

import jax
import jax.numpy as jnp
from jax import lax
from jax.experimental import pallas as pl
from jax.experimental.pallas import tpu as pltpu
from jax.sharding import PartitionSpec as P

MESH = pl.DeviceIdType.MESH
HD = 128
HEADS = 24
SPATIAL = 16
TEMPORAL = HEADS - SPATIAL
TILE = 128
TILES = 16
TOKENS = TILES * TILE
NEGATIVE = -1e30
EXPONENT = math.log2(math.e) / math.sqrt(HD)
CHUNK = 512
NT = (((1,), (1,)), ((), ()))
BF16 = jnp.bfloat16
F32 = jnp.float32

BAND_STEPS = (
    (0, 0), (1, 0), (0, 3), (3, 0), (0, 1), (2, 0), (0, 2), (1, 1),
    (3, 3), (1, 3), (3, 1), (2, 1), (1, 2), (2, 3), (3, 2), (2, 2),
)
FRAME_STEPS = ((0, 0), (0, 1), (1, 0), (3, 0), (1, 1), (3, 1), (2, 0), (2, 1))


def pick(table, index):
    if isinstance(index, int):
        return table[index]
    value = jnp.int32(table[0])
    for place in range(1, len(table)):
        value = jnp.where(index == place, jnp.int32(table[place]), value)
    return value


def when(condition, action):
    if isinstance(condition, bool):
        if condition:
            action()
    else:
        pl.when(condition)(action)


def band_at(me, index, sign):
    dx = pick([s[0] for s in BAND_STEPS], index)
    dy = pick([s[1] for s in BAND_STEPS], index)
    return (me // 4 + 4 + sign * dx) % 4 * 4 + (me % 4 + 4 + sign * dy) % 4


def frame_at(me, index, sign):
    dz = pick([s[0] for s in FRAME_STEPS], index)
    dc = pick([s[1] for s in FRAME_STEPS], index)
    return (me // 2 + 4 + sign * dz) % 4 * 2 + (me % 2 + dc) % 2


def score_tile(query, keys, marks, scores, tops):
    running = None
    for start in range(0, TOKENS, CHUNK):
        first = start // TILE
        key = keys[pl.ds(first, CHUNK // TILE), 0].reshape(CHUNK, HD)
        key = jnp.concatenate([key, marks[pl.ds(start, CHUNK), :]], axis=1)
        part = lax.dot_general(query, key, NT, preferred_element_type=F32)
        scores[:, pl.ds(start, CHUNK)] = part
        for lane in range(0, CHUNK, 128):
            piece = part[:, lane : lane + 128]
            running = piece if running is None else jnp.maximum(running, piece)
    top = jnp.max(running, axis=1, keepdims=True)
    tops[...] = jnp.broadcast_to(top, tops.shape)


def value_tile(scores, tops, values):
    top = jnp.concatenate([tops[...]] * (CHUNK // 128), axis=1)
    total = None
    ones = jnp.ones((CHUNK, HD), BF16)
    for start in range(0, TOKENS, CHUNK):
        first = start // TILE
        value = values[pl.ds(first, CHUNK // TILE), 1].reshape(CHUNK, HD)
        value = jnp.concatenate([value, ones], axis=1)
        weights = jnp.exp2((scores[:, pl.ds(start, CHUNK)] - top) * EXPONENT).astype(BF16)
        part = jnp.dot(weights, value, preferred_element_type=F32)
        total = part if total is None else total + part
    return (total[:, :HD] / total[:, HD:]).astype(BF16)


def kernel(
    q_hbm, k_hbm, v_hbm, ints_hbm,
    out,
    q_in, k_in, v_in, q_send, kv_send, qt_send, kvt_send, row_send,
    q_got, kv_got, row_got, o_send, o_got, marks,
    scores0, scores1, tops0, tops1, ints, place, order,
    load_sem, send_sem, kv_sem, row_sem, q_sem, o_sem, osend_sem, groups_in, all_in,
):
    group = lax.axis_index("frame")
    band = lax.axis_index("band")

    barrier = pltpu.get_barrier_semaphore()
    for i in range(1, 16):
        pl.semaphore_signal(barrier, inc=1, device_id={"band": band_at(band, i, 1)}, device_id_type=MESH)

    def greet_groups(sem):
        for i in range(1, 8):
            pl.semaphore_signal(sem, inc=1, device_id={"frame": frame_at(group, i, 1)}, device_id_type=MESH)

    pl.when(band == 0)(lambda: greet_groups(barrier))

    small = pltpu.make_async_copy(ints_hbm, ints, load_sem.at[3])
    small.start()
    def load(i, source, target):
        for h in range(HEADS):
            pltpu.make_async_copy(source.at[:, :, pl.ds(h * HD, HD)], target.at[h], load_sem.at[i]).start()
        return pltpu.make_async_copy(target, target, load_sem.at[i])

    k_load = load(0, k_hbm, k_in)
    v_load = load(1, v_hbm, v_in)
    small.wait()
    before = jnp.int32(0)
    counts = []
    for h in range(HEADS):
        here = ints[1, 2, h]
        place[h] = jnp.minimum(here * before + (1 - here) * (SPATIAL + h - before), HEADS - 1)
        before = before + here
        counts.append(before)

    def fill(slot, carry):
        spatial, temporal = jnp.int32(0), jnp.int32(0)
        for h in range(HEADS):
            spatial = spatial + (counts[h] <= slot).astype(jnp.int32)
            temporal = temporal + (h + 1 - counts[h] <= slot).astype(jnp.int32)
        order[slot] = jnp.minimum(spatial, HEADS - 1)

        @pl.when(slot < TEMPORAL)
        def _():
            order[SPATIAL + slot] = jnp.minimum(temporal, HEADS - 1)

        return carry

    lax.fori_loop(0, SPATIAL, fill, 0)

    lane = lax.broadcasted_iota(jnp.int32, (1, 128), 1)
    for kind in range(2):
        for f in range(2):
            row = jnp.zeros((1, 128), F32)
            for t in range(TILES):
                row = jnp.where(lane == t, (1 - ints[f, kind, t]).astype(F32) * NEGATIVE, row)
            row_send[kind, f] = row
            if kind == 0:
                row_got[f, band] = row
            else:
                row_got[2, 2 * group + f] = row

    def head(ref, f, slot):
        return ref[order[slot], f]

    def send(source, target, device, sent, got):
        pltpu.make_async_remote_copy(
            src_ref=source,
            dst_ref=target,
            send_sem=sent,
            recv_sem=got,
            device_id=device,
            device_id_type=MESH,
        ).start()

    def send_rows(kind):
        for i in range(1, 16 - 8 * kind):
            if kind == 0:
                target, device = row_got.at[pl.ds(0, 2), band], {"band": band_at(band, i, 1)}
            else:
                target, device = row_got.at[2, pl.ds(2 * group, 2)], {"frame": frame_at(group, i, 1)}
            send(row_send.at[kind], target, device, send_sem.at[2, kind], row_sem.at[kind])

    def keep_own(f):
        kv_got[f, band, 0] = head(k_in, f, band)
        kv_got[f, band, 1] = head(v_in, f, band)
        q_got[f, band] = head(q_in, f, band)
        kv_got[2, 2 * group + f, 0] = head(k_in, f, SPATIAL + group)
        kv_got[2, 2 * group + f, 1] = head(v_in, f, SPATIAL + group)
        q_got[2, 2 * group + f] = head(q_in, f, SPATIAL + group)

    def send_keys(f, places):
        for i in places:
            dest = band_at(band, i, 1)
            kv_send[f, i, 0] = head(k_in, f, dest)
            kv_send[f, i, 1] = head(v_in, f, dest)
            send(kv_send.at[f, i], kv_got.at[f, band], {"band": dest}, send_sem.at[0, f], kv_sem.at[f])

    def send_queries(f, places):
        for i in places:
            dest = band_at(band, i, 1)
            q_send[f, i] = head(q_in, f, dest)
            send(q_send.at[f, i], q_got.at[f, band], {"band": dest}, send_sem.at[1, f], q_sem.at[f, i])

    def send_temporal():
        for i in range(1, 8):
            dest = frame_at(group, i, 1)
            for f in range(2):
                kvt_send[i, f, 0] = head(k_in, f, SPATIAL + dest)
                kvt_send[i, f, 1] = head(v_in, f, SPATIAL + dest)
            send(kvt_send.at[i], kv_got.at[2, pl.ds(2 * group, 2)], {"frame": dest}, send_sem.at[0, 2], kv_sem.at[2])
        for i in range(1, 8):
            dest = frame_at(group, i, 1)
            for f in range(2):
                qt_send[i, f] = head(q_in, f, SPATIAL + dest)
            send(qt_send.at[i], q_got.at[2, pl.ds(2 * group, 2)], {"frame": dest}, send_sem.at[1, 2], q_sem.at[2, i])

    everyone = range(1, 16)
    q_load = load(2, q_hbm, q_in)
    k_load.wait()
    v_load.wait()
    pl.when(band > 0)(lambda: pl.semaphore_wait(barrier, 15))

    @pl.when(band == 0)
    def _():
        pl.semaphore_wait(barrier, 22)
        greet_groups(groups_in)

    send_keys(0, everyone)
    send_rows(0)
    q_load.wait()
    send_queries(0, everyone)

    @pl.when(band == 0)
    def _():
        pl.semaphore_wait(groups_in, 7)
        for i in range(1, 16):
            pl.semaphore_signal(all_in, inc=1, device_id={"band": band_at(band, i, 1)}, device_id_type=MESH)

    pl.when(band > 0)(lambda: pl.semaphore_wait(all_in, 1))
    send_temporal()
    send_rows(1)
    send_keys(1, everyone)
    send_queries(1, everyone)
    keep_own(0)
    keep_own(1)

    lane = lax.broadcasted_iota(jnp.int32, (TILE, 128), 1)
    for t in range(TILES):
        marks[pl.ds(t * TILE, TILE), :] = jnp.where(lane == t, 1.0, 0.0).astype(BF16)

    def wait_bytes(ref, sem):
        pltpu.make_async_copy(ref, ref, sem).wait()

    def wait_keys(u):
        many = 15 if u < 2 else 14
        wait_bytes(kv_got.at[u, pl.ds(0, many)], kv_sem.at[u])

    def tiles_of(u, step):
        if u < 2:
            return band_at(band, 2 * step, -1), band_at(band, 2 * step + 1, -1)
        source = frame_at(group, step, -1)
        return 2 * source, 2 * source + 1

    def wait_query(u, step):
        if u < 2:

            def first():
                wait_bytes(q_got.at[u, 0], q_sem.at[u, 2 * step])

            when(step > 0, first)

            wait_bytes(q_got.at[u, 0], q_sem.at[u, 2 * step + 1])
        else:

            when(step > 0, lambda: wait_bytes(q_got.at[u, pl.ds(0, 2)], q_sem.at[u, step]))

    def run_scores(u, step, scores, tops):
        rows = []
        for t in tiles_of(u, step):
            bias = jnp.broadcast_to(row_got[u, t], (TILE, 128)).astype(BF16)
            rows.append(jnp.concatenate([q_got[u, t], bias], axis=1))
        score_tile(jnp.concatenate(rows, axis=0), kv_got.at[u], marks, scores, tops)

    def run_values(u, step, scores, tops):
        result = value_tile(scores, tops, kv_got.at[u])
        first, second = tiles_of(u, step)
        o_send[u, first] = result[:TILE]
        o_send[u, second] = result[TILE:]
        if u == 0:
            return
        if u < 2:
            for t, guarded in ((first, True), (second, False)):
                copy = pltpu.make_async_remote_copy(
                    src_ref=o_send.at[u, t],
                    dst_ref=o_got.at[band, u],
                    send_sem=osend_sem.at[u],
                    recv_sem=o_sem.at[u],
                    device_id={"band": t},
                    device_id_type=MESH,
                )
                if guarded:
                    when(step > 0, copy.start)
                else:
                    copy.start()
        else:
            copy = pltpu.make_async_remote_copy(
                src_ref=o_send.at[2, pl.ds(first, 2)],
                dst_ref=o_got.at[SPATIAL + group],
                send_sem=osend_sem.at[u],
                recv_sem=o_sem.at[u],
                device_id={"frame": first // 2},
                device_id_type=MESH,
            )
            when(step > 0, copy.start)

    def run_unit(u):
        wait_keys(u)
        if u == 1:
            for i in range(1, 16):
                t = band_at(band, i, -1)
                pltpu.make_async_remote_copy(
                    src_ref=o_send.at[0, t],
                    dst_ref=o_got.at[band, 0],
                    send_sem=osend_sem.at[0],
                    recv_sem=o_sem.at[0],
                    device_id={"band": t},
                    device_id_type=MESH,
                ).start()
        wait_query(u, 0)
        run_scores(u, 0, scores0, tops0)

        def body(i, carry):
            wait_query(u, 2 * i + 1)
            run_scores(u, 2 * i + 1, scores1, tops1)
            run_values(u, 2 * i, scores0, tops0)

            wait_query(u, 2 * i + 2)
            run_scores(u, 2 * i + 2, scores0, tops0)
            run_values(u, 2 * i + 1, scores1, tops1)
            return carry

        lax.fori_loop(0, 3, body, 0)
        wait_query(u, 7)
        run_scores(u, 7, scores1, tops1)
        run_values(u, 6, scores0, tops0)
        run_values(u, 7, scores1, tops1)

    wait_bytes(row_got.at[pl.ds(0, 2), pl.ds(0, 15)], row_sem.at[0])
    run_unit(0)
    wait_bytes(row_got.at[2, pl.ds(0, 14)], row_sem.at[1])
    run_unit(2)
    run_unit(1)

    for f in range(2):
        o_got[band, f] = o_send[f, band]
        o_got[SPATIAL + group, f] = o_send[2, 2 * group + f]

    for f in range(2):
        wait_bytes(kv_send.at[f, pl.ds(1, 15)], send_sem.at[0, f])
        wait_bytes(q_send.at[f, pl.ds(1, 15)], send_sem.at[1, f])
    wait_bytes(kvt_send.at[pl.ds(1, 7)], send_sem.at[0, 2])
    wait_bytes(qt_send.at[pl.ds(1, 7)], send_sem.at[1, 2])
    wait_bytes(row_got.at[pl.ds(0, 2), pl.ds(0, 15)], send_sem.at[2, 0])
    wait_bytes(row_got.at[2, pl.ds(0, 14)], send_sem.at[2, 1])
    for u, many in ((0, 15), (1, 15), (2, 14)):
        wait_bytes(o_send.at[u, pl.ds(0, many)], osend_sem.at[u])
    for u, many in ((0, 15), (1, 15), (2, 14)):
        wait_bytes(o_send.at[u, pl.ds(0, many)], o_sem.at[u])

    for h in range(HEADS):
        for f in range(2):
            out[f, :, pl.ds(h * HD, HD)] = o_got[place[h], f]


def body(queries, keys, values, head_kind, spatial_mask, temporal_mask):
    vmem, sem = pltpu.VMEM, pltpu.SemaphoreType.DMA
    hbm = pl.BlockSpec(memory_space=pltpu.HBM)
    wide = HEADS - TILES
    ints = (
        jnp.pad(spatial_mask, ((0, 0), (0, 2), (0, wide)))
        + jnp.pad(temporal_mask.transpose(1, 0, 2), ((0, 0), (1, 1), (0, wide)))
        + jnp.pad(head_kind.reshape(1, 1, HEADS), ((1, 0), (2, 0), (0, 0)))
    )
    return pl.pallas_call(
        kernel,
        out_shape=jax.ShapeDtypeStruct(queries.shape, BF16),
        in_specs=[hbm] * 4,
        out_specs=pl.BlockSpec(memory_space=pltpu.VMEM),
        scratch_shapes=[
            vmem((HEADS, 2, TILE, HD), BF16), vmem((HEADS, 2, TILE, HD), BF16), vmem((HEADS, 2, TILE, HD), BF16),
            vmem((2, 16, TILE, HD), BF16), vmem((2, 16, 2, TILE, HD), BF16),
            vmem((8, 2, TILE, HD), BF16), vmem((8, 2, 2, TILE, HD), BF16), vmem((2, 2, 1, 128), F32),
            vmem((3, TILES, TILE, HD), BF16), vmem((3, TILES, 2, TILE, HD), BF16), vmem((3, TILES, 1, 128), F32),
            vmem((3, TILES, TILE, HD), BF16), vmem((HEADS, 2, TILE, HD), BF16),
            vmem((TOKENS, 128), BF16),
            vmem((256, TOKENS), F32), vmem((256, TOKENS), F32), vmem((256, 128), F32), vmem((256, 128), F32),
            pltpu.SMEM((2, 3, HEADS), jnp.int32),
            pltpu.SMEM((HEADS,), jnp.int32), pltpu.SMEM((HEADS,), jnp.int32),
            sem((4,)), sem((3, 3)), sem((3,)), sem((2,)), sem((3, 16)), sem((3,)), sem((3,)),
            pltpu.SemaphoreType.REGULAR, pltpu.SemaphoreType.REGULAR,
        ],
        compiler_params=pltpu.CompilerParams(
            collective_id=0, has_side_effects=True, vmem_limit_bytes=52 * 2**20
        ),
        cost_estimate=pl.CostEstimate(flops=6442450944, bytes_accessed=6291456, transcendentals=12582912),
    )(queries, keys, values, ints)


def solution(mesh):
    return jax.shard_map(
        body,
        mesh=mesh,
        in_specs=(
            P("frame", "band", None),
            P("frame", "band", None),
            P("frame", "band", None),
            P(),
            P("frame", "band", None),
            P("band", "frame", None),
        ),
        out_specs=P("frame", "band", None),
        check_vma=False,
    )
```

time: 65.4 us -> 58 us (0.89)
  local copies, waits for them, and re-layouts: 5.97 us -> 1.15 us
  Pallas kernels: 59 us -> 55.7 us
  other arithmetic: 0 us -> 0.72 us
    unnamed x11 -> x1, local copies, waits for them, and re-layouts: 5.97 us -> 1.15 us
    pallas_call x1, Pallas kernels: 59 us -> 55.7 us  [body(): pl.pallas_call(kernel, out_shape=jax.ShapeDtypeStruct(queries.shape, BF16...]
    add x0 -> x1, other arithmetic: none -> 0.72 us  [body(): jnp.pad(spatial_mask, ((0, 0), (0, 2), (0, wide)))]
where the time goes in v2:
time: 58 us; the launch traced here: 57.6 us
  Pallas kernels  55.7 us (96%)
  local copies, waits for them, and re-layouts  1.15 us (2%)
  other arithmetic  0.72 us (1%)
    pallas_call x1, Pallas kernels, body(): pl.pallas_call(kernel, out_shape=jax.ShapeDtypeStruct(queries.shape, BF16...  55.7 us

profile of v2, /device:TPU:0, one launch (start us, length us, event | category | flops | bytes accessed | tf_op | source)
XLA Modules:
  0.0 57.6 jit_solution(314532114019620623)
XLA Ops:
  0.0 0.7 %pad_add_fusion.ints_hbm = s32[2,3,24]{2,1,0:T(4,128)S(1)} fusion(s32[1,1,24]{2,1,0:T(1,128)} %bitcast.5, s32[2,1,16]{2,1,0:T(1,128)} %bitcast.4, s32[2,1,16]{2,1,0:T(1,128)} %param.10), kind=kLoop, calls=%fused_computation | loop fusion | flops 288 | bytes 928 | tf_op jit(solution)/shard_map/add | solution.py:375
  0.7 55.7 %shard_map.64 = bf16[2,128,3072]{2,1,0:T(8,128)(2,1)S(1)} custom-call(bf16[2,128,3072]{2,1,0:T(8,128)(2,1)} %q_hbm.1, bf16[2,128,3072]{2,1,0:T(8,128)(2,1)} %k_hbm.1, bf16[2,128,3072]{2,1,0:T(8,128)(2,1)} %v_hbm.1, s32[2,3,24]{2,1,0:T(4,128)S(1)} %pad_add_fusion.ints_hbm), custom_call_target="tpu_custom_call" | custom-call | flops 6442450944 | bytes 6291456 | tf_op jit(solution)/shard_map/pallas_call | solution.py:379
  56.4 1.1 %copy.9 = bf16[2,128,3072]{2,1,0:T(8,128)(2,1)} copy(bf16[2,128,3072]{2,1,0:T(8,128)(2,1)S(1)} %shard_map.64) | data formatting | bytes 3145728

commit v3 on v2

--- a/solution.py
+++ b/solution.py
@@ -103,11 +103,13 @@
     for i in range(1, 16):
         pl.semaphore_signal(barrier, inc=1, device_id={"band": band_at(band, i, 1)}, device_id_type=MESH)
 
+    leader = band % 4 == 0
+
     def greet_groups(sem):
         for i in range(1, 8):
             pl.semaphore_signal(sem, inc=1, device_id={"frame": frame_at(group, i, 1)}, device_id_type=MESH)
 
-    pl.when(band == 0)(lambda: greet_groups(barrier))
+    pl.when(leader)(lambda: greet_groups(barrier))
 
     small = pltpu.make_async_copy(ints_hbm, ints, load_sem.at[3])
     small.start()
@@ -213,9 +215,9 @@
     q_load = load(2, q_hbm, q_in)
     k_load.wait()
     v_load.wait()
-    pl.when(band > 0)(lambda: pl.semaphore_wait(barrier, 15))
-
-    @pl.when(band == 0)
+    pl.when(band % 4 > 0)(lambda: pl.semaphore_wait(barrier, 15))
+
+    @pl.when(leader)
     def _():
         pl.semaphore_wait(barrier, 22)
         greet_groups(groups_in)
@@ -225,13 +227,13 @@
     q_load.wait()
     send_queries(0, everyone)
 
-    @pl.when(band == 0)
+    @pl.when(leader)
     def _():
         pl.semaphore_wait(groups_in, 7)
-        for i in range(1, 16):
-            pl.semaphore_signal(all_in, inc=1, device_id={"band": band_at(band, i, 1)}, device_id_type=MESH)
-
-    pl.when(band > 0)(lambda: pl.semaphore_wait(all_in, 1))
+        for i in range(1, 4):
+            pl.semaphore_signal(all_in, inc=1, device_id={"band": band + i}, device_id_type=MESH)
+
+    pl.when(band % 4 > 0)(lambda: pl.semaphore_wait(all_in, 1))
     send_temporal()
     send_rows(1)
     send_keys(1, everyone)

time: 58 us -> 56.9 us (0.981)
  Pallas kernels: 55.7 us -> 54.8 us
    pallas_call x1, Pallas kernels: 55.7 us -> 54.8 us  [body(): pl.pallas_call(kernel, out_shape=jax.ShapeDtypeStruct(queries.shape, BF16...]
where the time goes in v3:
time: 56.9 us; the launch traced here: 56.7 us
  Pallas kernels  54.8 us (96%)
  local copies, waits for them, and re-layouts  1.15 us (2%)
  other arithmetic  0.72 us (1%)
    pallas_call x1, Pallas kernels, body(): pl.pallas_call(kernel, out_shape=jax.ShapeDtypeStruct(queries.shape, BF16...  54.8 us
    unnamed x1, local copies, waits for them, and re-layouts  1.15 us

profile of v3, /device:TPU:0, one launch (start us, length us, event | category | flops | bytes accessed | tf_op | source)
XLA Modules:
  0.0 56.7 jit_solution(13721540251018472139)
XLA Ops:
  0.0 0.7 %pad_add_fusion.ints_hbm = s32[2,3,24]{2,1,0:T(4,128)S(1)} fusion(s32[1,1,24]{2,1,0:T(1,128)} %bitcast.5, s32[2,1,16]{2,1,0:T(1,128)} %bitcast.4, s32[2,1,16]{2,1,0:T(1,128)} %param.10), kind=kLoop, calls=%fused_computation | loop fusion | flops 288 | bytes 928 | tf_op jit(solution)/shard_map/add | solution.py:377
  0.7 54.8 %shard_map.64 = bf16[2,128,3072]{2,1,0:T(8,128)(2,1)S(1)} custom-call(bf16[2,128,3072]{2,1,0:T(8,128)(2,1)} %q_hbm.1, bf16[2,128,3072]{2,1,0:T(8,128)(2,1)} %k_hbm.1, bf16[2,128,3072]{2,1,0:T(8,128)(2,1)} %v_hbm.1, s32[2,3,24]{2,1,0:T(4,128)S(1)} %pad_add_fusion.ints_hbm), custom_call_target="tpu_custom_call" | custom-call | flops 6442450944 | bytes 6291456 | tf_op jit(solution)/shard_map/pallas_call | solution.py:381
  55.6 1.1 %copy.9 = bf16[2,128,3072]{2,1,0:T(8,128)(2,1)} copy(bf16[2,128,3072]{2,1,0:T(8,128)(2,1)S(1)} %shard_map.64) | data formatting | bytes 3145728

commit v4 on v3

--- a/solution.py
+++ b/solution.py
@@ -92,15 +92,16 @@
     q_hbm, k_hbm, v_hbm, ints_hbm,
     out,
     q_in, k_in, v_in, q_send, kv_send, qt_send, kvt_send, row_send,
-    q_got, kv_got, row_got, o_send, o_got, marks,
+    q_got, kv_got, row_got, o_send, o_got0, o_got1, marks,
     scores0, scores1, tops0, tops1, ints, place, order,
     load_sem, send_sem, kv_sem, row_sem, q_sem, o_sem, osend_sem, groups_in, all_in,
 ):
+    o_got = (o_got0, o_got1)
     group = lax.axis_index("frame")
     band = lax.axis_index("band")
 
     barrier = pltpu.get_barrier_semaphore()
-    for i in range(1, 16):
+    for i in range(15, 0, -1):
         pl.semaphore_signal(barrier, inc=1, device_id={"band": band_at(band, i, 1)}, device_id_type=MESH)
 
     leader = band % 4 == 0
@@ -289,7 +290,7 @@
             for t, guarded in ((first, True), (second, False)):
                 copy = pltpu.make_async_remote_copy(
                     src_ref=o_send.at[u, t],
-                    dst_ref=o_got.at[band, u],
+                    dst_ref=o_got[u].at[band],
                     send_sem=osend_sem.at[u],
                     recv_sem=o_sem.at[u],
                     device_id={"band": t},
@@ -300,15 +301,16 @@
                 else:
                     copy.start()
         else:
-            copy = pltpu.make_async_remote_copy(
-                src_ref=o_send.at[2, pl.ds(first, 2)],
-                dst_ref=o_got.at[SPATIAL + group],
-                send_sem=osend_sem.at[u],
-                recv_sem=o_sem.at[u],
-                device_id={"frame": first // 2},
-                device_id_type=MESH,
-            )
-            when(step > 0, copy.start)
+            for f in range(2):
+                copy = pltpu.make_async_remote_copy(
+                    src_ref=o_send.at[2, first + f],
+                    dst_ref=o_got[f].at[SPATIAL + group],
+                    send_sem=osend_sem.at[u],
+                    recv_sem=o_sem.at[u],
+                    device_id={"frame": first // 2},
+                    device_id_type=MESH,
+                )
+                when(step > 0, copy.start)
 
     def run_unit(u):
         wait_keys(u)
@@ -317,7 +319,7 @@
                 t = band_at(band, i, -1)
                 pltpu.make_async_remote_copy(
                     src_ref=o_send.at[0, t],
-                    dst_ref=o_got.at[band, 0],
+                    dst_ref=o_got0.at[band],
                     send_sem=osend_sem.at[0],
                     recv_sem=o_sem.at[0],
                     device_id={"band": t},
@@ -349,8 +351,14 @@
     run_unit(1)
 
     for f in range(2):
-        o_got[band, f] = o_send[f, band]
-        o_got[SPATIAL + group, f] = o_send[2, 2 * group + f]
+        o_got[f][band] = o_send[f, band]
+        o_got[f][SPATIAL + group] = o_send[2, 2 * group + f]
+
+    wait_bytes(o_send.at[2, pl.ds(0, 14)], o_sem.at[2])
+    for f in range(2):
+        wait_bytes(o_send.at[f, pl.ds(0, 15)], o_sem.at[f])
+        for h in range(HEADS):
+            out[f, :, pl.ds(h * HD, HD)] = o_got[f][place[h]]
 
     for f in range(2):
         wait_bytes(kv_send.at[f, pl.ds(1, 15)], send_sem.at[0, f])
@@ -361,12 +369,6 @@
     wait_bytes(row_got.at[2, pl.ds(0, 14)], send_sem.at[2, 1])
     for u, many in ((0, 15), (1, 15), (2, 14)):
         wait_bytes(o_send.at[u, pl.ds(0, many)], osend_sem.at[u])
-    for u, many in ((0, 15), (1, 15), (2, 14)):
-        wait_bytes(o_send.at[u, pl.ds(0, many)], o_sem.at[u])
-
-    for h in range(HEADS):
-        for f in range(2):
-            out[f, :, pl.ds(h * HD, HD)] = o_got[place[h], f]
 
 
 def body(queries, keys, values, head_kind, spatial_mask, temporal_mask):
@@ -388,7 +390,7 @@
             vmem((2, 16, TILE, HD), BF16), vmem((2, 16, 2, TILE, HD), BF16),
             vmem((8, 2, TILE, HD), BF16), vmem((8, 2, 2, TILE, HD), BF16), vmem((2, 2, 1, 128), F32),
             vmem((3, TILES, TILE, HD), BF16), vmem((3, TILES, 2, TILE, HD), BF16), vmem((3, TILES, 1, 128), F32),
-            vmem((3, TILES, TILE, HD), BF16), vmem((HEADS, 2, TILE, HD), BF16),
+            vmem((3, TILES, TILE, HD), BF16), vmem((HEADS, TILE, HD), BF16), vmem((HEADS, TILE, HD), BF16),
             vmem((TOKENS, 128), BF16),
             vmem((256, TOKENS), F32), vmem((256, TOKENS), F32), vmem((256, 128), F32), vmem((256, 128), F32),
             pltpu.SMEM((2, 3, HEADS), jnp.int32),

time: 56.9 us -> 56.7 us (level)
  no operation moved by 1% of the time
where the time goes in v4:
time: 56.7 us; the launch traced here: 56.5 us
  Pallas kernels  54.6 us (96%)
  local copies, waits for them, and re-layouts  1.15 us (2%)
  other arithmetic  0.72 us (1%)
    pallas_call x1, Pallas kernels, body(): pl.pallas_call(kernel, out_shape=jax.ShapeDtypeStruct(queries.shape, BF16...  54.6 us
    unnamed x1, local copies, waits for them, and re-layouts  1.15 us

profile of v4, /device:TPU:0, one launch (start us, length us, event | category | flops | bytes accessed | tf_op | source)
XLA Modules:
  0.0 56.5 jit_solution(16371243175387880672)
XLA Ops:
  0.0 0.7 %pad_add_fusion.ints_hbm = s32[2,3,24]{2,1,0:T(4,128)S(1)} fusion(s32[1,1,24]{2,1,0:T(1,128)} %bitcast.5, s32[2,1,16]{2,1,0:T(1,128)} %bitcast.4, s32[2,1,16]{2,1,0:T(1,128)} %param.10), kind=kLoop, calls=%fused_computation | loop fusion | flops 288 | bytes 928 | tf_op jit(solution)/shard_map/add | solution.py:379
  0.7 54.6 %shard_map.64 = bf16[2,128,3072]{2,1,0:T(8,128)(2,1)S(1)} custom-call(bf16[2,128,3072]{2,1,0:T(8,128)(2,1)} %q_hbm.1, bf16[2,128,3072]{2,1,0:T(8,128)(2,1)} %k_hbm.1, bf16[2,128,3072]{2,1,0:T(8,128)(2,1)} %v_hbm.1, s32[2,3,24]{2,1,0:T(4,128)S(1)} %pad_add_fusion.ints_hbm), custom_call_target="tpu_custom_call" | custom-call | flops 6442450944 | bytes 6291456 | tf_op jit(solution)/shard_map/pallas_call | solution.py:383
  55.3 1.1 %copy.9 = bf16[2,128,3072]{2,1,0:T(8,128)(2,1)} copy(bf16[2,128,3072]{2,1,0:T(8,128)(2,1)S(1)} %shard_map.64) | data formatting | bytes 3145728

commit v5 on v4

--- a/solution.py
+++ b/solution.py
@@ -24,8 +24,8 @@
 F32 = jnp.float32
 
 BAND_STEPS = (
-    (0, 0), (1, 0), (0, 3), (3, 0), (0, 1), (2, 0), (0, 2), (1, 1),
-    (3, 3), (1, 3), (3, 1), (2, 1), (1, 2), (2, 3), (3, 2), (2, 2),
+    (0, 0), (1, 0), (2, 1), (3, 3), (0, 3), (1, 2), (3, 1), (2, 0),
+    (3, 0), (2, 3), (1, 1), (0, 1), (3, 2), (1, 3), (0, 2), (2, 2),
 )
 FRAME_STEPS = ((0, 0), (0, 1), (1, 0), (3, 0), (1, 1), (3, 1), (2, 0), (2, 1))
 
@@ -313,7 +313,6 @@
                 when(step > 0, copy.start)
 
     def run_unit(u):
-        wait_keys(u)
         if u == 1:
             for i in range(1, 16):
                 t = band_at(band, i, -1)
@@ -325,6 +324,7 @@
                     device_id={"band": t},
                     device_id_type=MESH,
                 ).start()
+        wait_keys(u)
         wait_query(u, 0)
         run_scores(u, 0, scores0, tops0)
 

time: 56.7 us -> 56.9 us (level)
  no operation moved by 1% of the time
where the time goes in v5:
time: 56.9 us; the launch traced here: 56.6 us
  Pallas kernels  54.7 us (96%)
  local copies, waits for them, and re-layouts  1.15 us (2%)
  other arithmetic  0.72 us (1%)
    pallas_call x1, Pallas kernels, body(): pl.pallas_call(kernel, out_shape=jax.ShapeDtypeStruct(queries.shape, BF16...  54.7 us
    unnamed x1, local copies, waits for them, and re-layouts  1.15 us

profile of v5, /device:TPU:0, one launch (start us, length us, event | category | flops | bytes accessed | tf_op | source)
XLA Modules:
  0.0 56.6 jit_solution(1753127014880354054)
XLA Ops:
  0.0 0.7 %pad_add_fusion.ints_hbm = s32[2,3,24]{2,1,0:T(4,128)S(1)} fusion(s32[1,1,24]{2,1,0:T(1,128)} %bitcast.5, s32[2,1,16]{2,1,0:T(1,128)} %bitcast.4, s32[2,1,16]{2,1,0:T(1,128)} %param.10), kind=kLoop, calls=%fused_computation | loop fusion | flops 288 | bytes 928 | tf_op jit(solution)/shard_map/add | solution.py:379
  0.7 54.7 %shard_map.64 = bf16[2,128,3072]{2,1,0:T(8,128)(2,1)S(1)} custom-call(bf16[2,128,3072]{2,1,0:T(8,128)(2,1)} %q_hbm.1, bf16[2,128,3072]{2,1,0:T(8,128)(2,1)} %k_hbm.1, bf16[2,128,3072]{2,1,0:T(8,128)(2,1)} %v_hbm.1, s32[2,3,24]{2,1,0:T(4,128)S(1)} %pad_add_fusion.ints_hbm), custom_call_target="tpu_custom_call" | custom-call | flops 6442450944 | bytes 6291456 | tf_op jit(solution)/shard_map/pallas_call | solution.py:383
  55.4 1.1 %copy.9 = bf16[2,128,3072]{2,1,0:T(8,128)(2,1)} copy(bf16[2,128,3072]{2,1,0:T(8,128)(2,1)S(1)} %shard_map.64) | data formatting | bytes 3145728
